TPU v7x, 512 devices: a whole 4x4x16 slice. The times are simulated.
512 devices in a mesh: segment: 8 (over y, core), vocab: 64 (over z, x).
Axes of the slice: x: 4, y: 4, z: 16, core: 2. Of those that a mesh axis runs over, the one named last changes fastest.
Arguments:
- hidden: bfloat16 [16384, 8192], P('vocab', 'segment'), may hold values from -160 to 160
- norm_gain: float32 [8192], P('segment'), may hold values from 0.5 to 1.5
- head: bfloat16 [65536, 8192], P('vocab', 'segment'), may hold values from -3 to 3
- allowed: int32 [4, 16384], P(None, 'vocab'), may hold values from 0 to 127, as said below
- target_slot: int32 [16384], P('vocab'), may hold values from 0 to 3
- target_offset: int32 [16384], P('vocab'), may hold values from 0 to 511
Outputs:
- logprob: float32 [16384], P('vocab')
Inputs may be any that keep to these rules, and one draw needn't show every extreme that they name: `allowed`: the 4 blocks of a token are distinct. Among the 256 tokens of one index of vocab, a block is named by at most 16 of them; in every draw some block is named by exactly 16 tokens of every index of vocab.
All inputs are finite; a program needn't handle non-finite values.
Results may differ from a plain program's by a relative error of at most 0.00083.
Values may be sent and summed in bfloat16 or wider, within the bound.
A program may use at most 64 MiB of HBM per device.

v0:
```python
import jax
import jax.numpy as jnp
from jax import lax
from jax.sharding import PartitionSpec as P

D = 8192
BLOCK = 512
A = 4


def block_stats(logits, targets):
    peak_value = jnp.max(logits, axis=-1)
    exp_total = jnp.sum(jnp.exp(logits - peak_value[..., None]), axis=-1)
    column = lax.broadcasted_iota(jnp.int32, logits.shape, logits.ndim - 1)
    target_logit = jnp.sum(
        jnp.where(column == targets[..., None], logits, jnp.zeros_like(logits)), axis=-1
    )
    return (peak_value, exp_total, target_logit)


def per_device(hidden, norm_gain, head, allowed, target_slot, target_offset):
    tok_count = hidden.shape[0]
    slab_width = hidden.shape[1]
    vocab_size = lax.axis_size("vocab")
    blk_dev = head.shape[0] // BLOCK
    blk_count = blk_dev * vocab_size
    capacity = 2 * tok_count * A // blk_count
    widened = hidden.astype(jnp.float32)
    squares = lax.psum(jnp.sum(widened * widened, axis=1), "segment")
    normed = (widened * lax.rsqrt(squares / D + 1e-05)[:, None] * norm_gain[None, :]).astype(
        jnp.bfloat16
    )
    entries = allowed.reshape(-1)
    onehot = (entries[:, None] == jnp.arange(blk_count, dtype=jnp.int32)[None, :]).astype(jnp.int32)
    before = jnp.cumsum(onehot, axis=0) - onehot
    position = jnp.sum(before * onehot, axis=1)
    slot_index = entries * capacity + position
    slot_total = blk_count * capacity
    entry_token = jnp.tile(jnp.arange(tok_count, dtype=jnp.int32), A)
    slot_token = jnp.full((slot_total,), tok_count, jnp.int32).at[slot_index].set(entry_token)
    entry_choice = jnp.repeat(jnp.arange(A, dtype=jnp.int32), tok_count)
    entry_target = jnp.where(
        entry_choice == jnp.tile(target_slot, A), jnp.tile(target_offset, A), -1
    )
    slot_target = jnp.full((slot_total,), -1, jnp.int32).at[slot_index].set(entry_target)
    padded = jnp.concatenate([normed, jnp.zeros((1, slab_width), jnp.bfloat16)], axis=0)
    outgoing = padded[slot_token].reshape(vocab_size, blk_dev, capacity, slab_width)
    incoming, wanted = (
        lax.all_to_all(outgoing, "vocab", split_axis=0, concat_axis=0, tiled=True),
        lax.all_to_all(
            slot_target.reshape(vocab_size, blk_dev, capacity),
            "vocab",
            split_axis=0,
            concat_axis=0,
            tiled=True,
        ),
    )
    weights = head.reshape(blk_dev, BLOCK, slab_width)
    logits = lax.psum(
        jnp.einsum("sbcd,bvd->sbcv", incoming, weights, preferred_element_type=jnp.float32),
        "segment",
    )
    peak_value, exp_total, target_logit = block_stats(logits, wanted)
    peak_value, exp_total, target_logit = (
        lax.all_to_all(peak_value, "vocab", split_axis=0, concat_axis=0, tiled=True),
        lax.all_to_all(exp_total, "vocab", split_axis=0, concat_axis=0, tiled=True),
        lax.all_to_all(target_logit, "vocab", split_axis=0, concat_axis=0, tiled=True),
    )
    peak_value = peak_value.reshape(-1)[slot_index].reshape(A, tok_count)
    exp_total = exp_total.reshape(-1)[slot_index].reshape(A, tok_count)
    target_logit = target_logit.reshape(-1)[slot_index].reshape(A, tok_count)
    largest = jnp.max(peak_value, axis=0)
    log_total = largest + jnp.log(
        jnp.sum(exp_total * jnp.exp(peak_value - largest[None, :]), axis=0)
    )
    return jnp.sum(target_logit, axis=0) - log_total


def solution(mesh):
    return jax.shard_map(
        per_device,
        mesh=mesh,
        in_specs=(
            P("vocab", "segment"),
            P("segment"),
            P("vocab", "segment"),
            P(None, "vocab"),
            P("vocab"),
            P("vocab"),
        ),
        out_specs=P("vocab"),
        check_vma=False,
    )
```

profile of v0, /device:TPU:2, one launch (start us, length us, event | category | flops | bytes accessed | tf_op | source)
XLA Modules:
  0.0 419.9 jit_solution(16631843202107226767)
XLA Ops:
  6.5 0.0 copy-start
  6.5 0.0 copy-start.1
  6.5 0.0 all-reduce.3.cloned.1.call-start
  6.5 0.8 eq.41
  7.4 0.7 multiply_bitcast_fusion
  8.1 0.1 copy.27
  8.2 0.2 fusion.10
  8.5 0.1 copy.28
  8.6 0.7 copy.36
  9.3 0.4 fusion.9
  9.7 4.3 %scatter_custom_fusion.1 = s32[2048]{0:T(1024)S(1)} fusion(s32[1024]{0:T(1024)S(1)} %bitcast.39, s32[1024]{0:T(1024)S(1)} %bitcast.43, s32[]{:T(128)} %constant.7.clone.1), kind=kCustom, calls=%fused_computation.32 | custom fusion | bytes 8196 | tf_op jit(solution)/shard_map/scatter | solution.py:40
  14.0 1.2 fusion.5
  15.2 14.9 %psum.14 = f32[256]{0:T(256)S(1)} all-reduce(f32[256]{0:T(256)S(1)} %fusion.5), channel_id=1, replica_groups=mesh['segment'=8,'vocab'=64] {'segment'}, use_global_device_ids=true, to_apply=%region_5.6 | all-reduce | flops 256 | bytes 2048 | tf_op jit(solution)/shard_map/psum | solution.py:29
  30.1 0.0 copy-done.1
  30.1 0.9 fusion.7
  31.0 9.7 %gather_fusion = bf16[2048,1024]{1,0:T(8,128)(2,1)} fusion(bf16[257,1024]{1,0:T(8,128)(2,1)S(1)} %concatenate.3, s32[2048]{0:T(1024)S(1)} %fusion.13), kind=kCustom, calls=%fused_computation | custom fusion | bytes 8396800 | tf_op jit(solution)/shard_map/gather | solution.py:47
  40.7 206.4 %all_to_all.25 = bf16[64,2,16,1024]{3,2,1,0:T(8,128)(2,1)S(1)} all-to-all(bf16[64,2,16,1024]{3,2,1,0:T(8,128)(2,1)} %bitcast.35), channel_id=1, replica_groups=mesh['segment'=8,'vocab'=64] {'vocab'}, dimensions={0} | all-to-all | bytes 8388608 | tf_op jit(solution)/shard_map/all_to_all | solution.py:49
  247.1 0.0 copy-done
  247.1 4.3 %fusion.2 = f32[64,2,16,512]{3,2,0,1:T(8,128)} fusion(bf16[2,512,1024,1]{2,1,3,0:T(8,128)(2,1)S(1)} %bitcast.34, bf16[64,2,16,1024]{3,2,1,0:T(8,128)(2,1)S(1)} %all_to_all.25), kind=kOutput, calls=%fused_computation.11 | convolution fusion | flops 2147483648 | bytes 10485760 | tf_op jit(solution)/shard_map/sbcd,bvd->sbcv/dot_general | solution.py:60
  251.5 0.0 copy-start.2
  251.5 0.0 copy-start.3
  251.5 0.0 all-reduce.3.cloned.1.call-update
  251.5 0.7 copy-done.2
  252.1 0.0 copy-done.3
  252.2 4.3 %scatter_custom_fusion = s32[2048]{0:T(1024)S(1)} fusion(s32[1024]{0:T(1024)S(1)} %bitcast.40, s32[1024]{0:T(1024)S(1)} %bitcast.44, s32[]{:T(128)} %constant.11.clone.1), kind=kCustom, calls=%fused_computation.37 | custom fusion | bytes 8196 | tf_op jit(solution)/shard_map/scatter | solution.py:45
  256.5 0.1 reshape.85
  256.6 19.9 %all_to_all.26 = s32[64,2,16]{2,1,0:T(2,128)S(1)} all-to-all(s32[64,2,16]{2,1,0:T(2,128)S(1)} %reshape.85), channel_id=1, replica_groups=mesh['segment'=8,'vocab'=64] {'vocab'}, dimensions={0} | all-to-all | bytes 16384 | tf_op jit(solution)/shard_map/all_to_all | solution.py:50
  276.5 53.9 %all-reduce.3.cloned.1.call-done = f32[64,2,16,512]{3,2,0,1:T(8,128)} async-done(((f32[64,2,16,512]{3,2,0,1:T(8,128)}), f32[64,2,16,512]{3,2,0,1:T(8,128)}) %all-reduce.3.cloned.1.call-update) | async-done | bytes 4194320 | tf_op jit(solution)/shard_map/psum | solution.py:59
  330.4 2.5 reduce_max.18
  332.9 3.2 exponential_reduce_fusion
  336.1 0.7 copy.33
  336.7 15.7 %all-to-all-start.4 = ((f32[64,2,16]{2,1,0:T(2,128)}), f32[64,2,16]{2,1,0:T(2,128)S(1)}, u32[]{:S(2)}, u32[]{:S(2)}) async-start(f32[64,2,16]{2,1,0:T(2,128)} %copy.33), calls=%async_computation.4 | async-start | bytes 131072 | tf_op jit(solution)/shard_map/all_to_all | solution.py:66
  352.4 0.7 copy.32
  353.1 13.5 %all-to-all-done.4 = f32[64,2,16]{2,1,0:T(2,128)S(1)} async-done(((f32[64,2,16]{2,1,0:T(2,128)}), f32[64,2,16]{2,1,0:T(2,128)S(1)}, u32[]{:S(2)}, u32[]{:S(2)}) %all-to-all-start.4) | async-done | bytes 8224 | tf_op jit(solution)/shard_map/all_to_all | solution.py:66
  366.6 5.6 %all-to-all-start.3 = ((f32[64,2,16]{2,1,0:T(2,128)}), f32[64,2,16]{2,1,0:T(2,128)S(1)}, u32[]{:S(2)}, u32[]{:S(2)}) async-start(f32[64,2,16]{2,1,0:T(2,128)} %copy.32), calls=%async_computation.3 | async-start | bytes 131072 | tf_op jit(solution)/shard_map/all_to_all | solution.py:65
  372.2 0.7 copy.31
  372.9 13.6 %all-to-all-done.3 = f32[64,2,16]{2,1,0:T(2,128)S(1)} async-done(((f32[64,2,16]{2,1,0:T(2,128)}), f32[64,2,16]{2,1,0:T(2,128)S(1)}, u32[]{:S(2)}, u32[]{:S(2)}) %all-to-all-start.3) | async-done | bytes 8224 | tf_op jit(solution)/shard_map/all_to_all | solution.py:65
  386.4 5.5 %all-to-all-start.2 = ((f32[64,2,16]{2,1,0:T(2,128)}), f32[64,2,16]{2,1,0:T(2,128)S(1)}, u32[]{:S(2)}, u32[]{:S(2)}) async-start(f32[64,2,16]{2,1,0:T(2,128)} %copy.31), calls=%async_computation.2 | async-start | bytes 131072 | tf_op jit(solution)/shard_map/all_to_all | solution.py:67
  392.0 0.1 reshape.92
  392.1 6.2 %gather_fusion.3 = f32[1024]{0:T(1024)S(1)} fusion(f32[2048]{0:T(1024)S(1)} %reshape.92, s32[1024]{0:T(1024)S(1)} %broadcast_clamp_fusion), kind=kCustom, calls=%fused_computation.3 | custom fusion | bytes 12288 | tf_op jit(solution)/shard_map/gather | solution.py:70
  398.3 0.1 reshape.90
  398.4 6.2 %gather_fusion.2 = f32[1024]{0:T(1024)S(1)} fusion(f32[2048]{0:T(1024)S(1)} %reshape.90, s32[1024]{0:T(1024)S(1)} %broadcast_clamp_fusion), kind=kCustom, calls=%fused_computation.2 | custom fusion | bytes 12288 | tf_op jit(solution)/shard_map/gather | solution.py:69
  404.6 1.5 all-to-all-done.2
  406.1 0.1 reshape.88
  406.2 6.2 %gather_fusion.1 = f32[1024]{0:T(1024)S(1)} fusion(f32[2048]{0:T(1024)S(1)} %reshape.88, s32[1024]{0:T(1024)S(1)} %broadcast_clamp_fusion), kind=kCustom, calls=%fused_computation.1 | custom fusion | bytes 12288 | tf_op jit(solution)/shard_map/gather | solution.py:71
  412.5 0.6 add_subtract_fusion
  (21 shorter events, 0.3 us)
Async XLA Ops:
  6.5 240.6 %copy-start = (bf16[1024,1024]{1,0:T(8,128)(2,1)S(1)}, bf16[1024,1024]{1,0:T(8,128)(2,1)}, u32[]{:S(2)}) copy-start(bf16[1024,1024]{1,0:T(8,128)(2,1)} %param.8) | copy-start | bytes 6291460
  6.5 23.6 %copy-start.1 = (bf16[256,1024]{1,0:T(8,128)(2,1)S(1)}, bf16[256,1024]{1,0:T(8,128)(2,1)}, u32[]{:S(2)}) copy-start(bf16[256,1024]{1,0:T(8,128)(2,1)} %param.6) | copy-start | bytes 1572868
  6.5 323.8 %all-reduce.3.cloned.1.call-start = ((), (), s32[]{:S(2)}) async-start(), calls=%async_computation.5 | async-start | bytes 8388608 | tf_op jit(solution)/shard_map/psum | solution.py:59
  251.5 0.7 copy-start.2
  251.5 0.7 copy-start.3
  336.7 29.9 %all-to-all-start.4 = ((f32[64,2,16]{2,1,0:T(2,128)}), f32[64,2,16]{2,1,0:T(2,128)S(1)}, u32[]{:S(2)}, u32[]{:S(2)}) async-start(f32[64,2,16]{2,1,0:T(2,128)} %copy.33), calls=%async_computation.4 | async-start | bytes 131072 | tf_op jit(solution)/shard_map/all_to_all | solution.py:66
  366.6 19.8 %all-to-all-start.3 = ((f32[64,2,16]{2,1,0:T(2,128)}), f32[64,2,16]{2,1,0:T(2,128)S(1)}, u32[]{:S(2)}, u32[]{:S(2)}) async-start(f32[64,2,16]{2,1,0:T(2,128)} %copy.32), calls=%async_computation.3 | async-start | bytes 131072 | tf_op jit(solution)/shard_map/all_to_all | solution.py:65
  386.4 19.7 %all-to-all-start.2 = ((f32[64,2,16]{2,1,0:T(2,128)}), f32[64,2,16]{2,1,0:T(2,128)S(1)}, u32[]{:S(2)}, u32[]{:S(2)}) async-start(f32[64,2,16]{2,1,0:T(2,128)} %copy.31), calls=%async_computation.2 | async-start | bytes 131072 | tf_op jit(solution)/shard_map/all_to_all | solution.py:67
Sparse Core Ops, SparseCore 0:
  251.6 78.7 all-reduce.2
where the time goes:
time: 420 us
  blocking collectives  241 us (57%)
  waiting for transfers between devices  82.5 us (20%)
  local copies, waits for them, and re-layouts  41.8 us (10%)
  starting transfers between devices  26.8 us (6%)
  between operations  13.6 us (3%)
  other arithmetic  9.78 us (2%)
  matrix products  4.34 us (1%)
    all_to_all x1, blocking collectives, per_device(): lax.all_to_all(outgoing, 'vocab', split_axis=0, concat_axis=0, tiled=True)  206 us
    psum x1, waiting for transfers between devices, per_device(): lax.psum(jnp.einsum('sbcd,bvd->sbcv', incoming, weights, preferred_elemen...  53.9 us
    all_to_all x1, blocking collectives, per_device(): lax.all_to_all(slot_target.reshape(vocab_size, blk_dev, capacity), 'vocab...  19.9 us
    all_to_all x1, starting transfers between devices, per_device(): lax.all_to_all(exp_total, 'vocab', split_axis=0, concat_axis=0, tiled=True)  15.7 us
    psum x1, blocking collectives, per_device(): squares = lax.psum(jnp.sum(widened * widened, axis=1), 'segment')  14.9 us
    all_to_all x1, waiting for transfers between devices, per_device(): lax.all_to_all(peak_value, 'vocab', split_axis=0, concat_axis=0, tiled=True)  13.6 us
    all_to_all x1, waiting for transfers between devices, per_device(): lax.all_to_all(exp_total, 'vocab', split_axis=0, concat_axis=0, tiled=True)  13.5 us
    gather x1, local copies, waits for them, and re-layouts, per_device(): padded[slot_token].reshape(vocab_size, blk_dev, capacity, slab_width)  9.67 us
  transfers between devices with their start and end apart: 4, of which 4 were waited for; matrix products, arithmetic and copies ran while one was open for 4% of the time, Pallas kernels for 0%

commit v1 on v0

--- a/solution.py
+++ b/solution.py
@@ -6,6 +6,12 @@
 D = 8192
 BLOCK = 512
 A = 4
+
+
+def summed_here(x, axis):
+    blocks = lax.all_gather(x, axis, axis=0, tiled=False)
+    total = blocks.sum(axis=0)
+    return total
 
 
 def block_stats(logits, targets):
@@ -56,7 +62,7 @@
         ),
     )
     weights = head.reshape(blk_dev, BLOCK, slab_width)
-    logits = lax.psum(
+    logits = summed_here(
         jnp.einsum("sbcd,bvd->sbcv", incoming, weights, preferred_element_type=jnp.float32),
         "segment",
     )

time: 420 us -> 513 us (1.22)
  the two profiles are of different devices: /device:TPU:2 before, /device:TPU:8 now
where the time goes in v1:
time: 513 us; the launch traced here: 512 us
  blocking collectives  240 us (47%)
  waiting for transfers between devices  163 us (32%)
  local copies, waits for them, and re-layouts  41.8 us (8%)
  starting transfers between devices  25 us (5%)
  other arithmetic  24.9 us (5%)
  between operations  13.6 us (3%)
    all_to_all x1, blocking collectives, per_device(): lax.all_to_all(outgoing, 'vocab', split_axis=0, concat_axis=0, tiled=True)  204 us
    all_gather x1, waiting for transfers between devices, summed_here(): blocks = lax.all_gather(x, axis, axis=0, tiled=False)  131 us
    all_to_all x1, blocking collectives, per_device(): lax.all_to_all(slot_target.reshape(vocab_size, blk_dev, capacity), 'vocab...  20.9 us
    all_to_all x1, starting transfers between devices, per_device(): lax.all_to_all(exp_total, 'vocab', split_axis=0, concat_axis=0, tiled=True)  15.6 us
    reduce_sum x1, other arithmetic, summed_here(): total = blocks.sum(axis=0)  15.1 us
    all_to_all x1, waiting for transfers between devices, per_device(): lax.all_to_all(exp_total, 'vocab', split_axis=0, concat_axis=0, tiled=True)  14.8 us
    psum x1, blocking collectives, per_device(): squares = lax.psum(jnp.sum(widened * widened, axis=1), 'segment')  14.8 us
    all_to_all x1, waiting for transfers between devices, per_device(): lax.all_to_all(peak_value, 'vocab', split_axis=0, concat_axis=0, tiled=True)  14.6 us
  transfers between devices with their start and end apart: 4, of which 4 were waited for; matrix products, arithmetic and copies ran while one was open for 4% of the time, Pallas kernels for 0%

profile of v1, /device:TPU:8, one launch (start us, length us, event | category | flops | bytes accessed | tf_op | source)
XLA Modules:
  0.0 512.0 jit_solution(9575952722907549198)
XLA Ops:
  6.5 0.0 copy-start
  6.5 0.0 copy-start.1
  6.5 0.0 all-gather.3.cloned.1.call-start
  6.5 0.8 eq.41
  7.4 0.7 multiply_bitcast_fusion
  8.1 0.1 copy.30
  8.2 0.2 fusion.10
  8.5 0.1 copy.31
  8.6 0.7 copy.39
  9.3 0.4 fusion.9
  9.7 4.3 scatter_custom_fusion.1
  14.0 1.2 fusion.5
  15.2 14.8 %psum.7 = f32[256]{0:T(256)S(1)} all-reduce(f32[256]{0:T(256)S(1)} %fusion.5), channel_id=1, replica_groups=mesh['segment'=8,'vocab'=64] {'segment'}, use_global_device_ids=true, to_apply=%region_5.6 | all-reduce | flops 256 | bytes 2048 | tf_op jit(solution)/shard_map/psum | solution.py:35
  30.0 0.0 copy-done.1
  30.0 0.9 fusion.7
  30.9 9.7 %gather_fusion = bf16[2048,1024]{1,0:T(8,128)(2,1)} fusion(bf16[257,1024]{1,0:T(8,128)(2,1)S(1)} %concatenate.3, s32[2048]{0:T(1024)S(1)} %fusion.13), kind=kCustom, calls=%fused_computation | custom fusion | bytes 8396800 | tf_op jit(solution)/shard_map/gather | solution.py:53
  40.6 203.9 %all_to_all.25 = bf16[64,2,16,1024]{3,2,1,0:T(8,128)(2,1)S(1)} all-to-all(bf16[64,2,16,1024]{3,2,1,0:T(8,128)(2,1)} %bitcast.37), channel_id=1, replica_groups=mesh['segment'=8,'vocab'=64] {'vocab'}, dimensions={0} | all-to-all | bytes 8388608 | tf_op jit(solution)/shard_map/all_to_all | solution.py:55
  244.6 0.0 copy-done
  244.6 4.4 fusion.2
  249.0 0.0 copy-start.2
  249.0 0.0 copy-start.3
  249.0 0.0 all-gather.3.cloned.1.call-update
  249.0 0.7 copy-done.2
  249.7 0.0 copy-done.3
  249.7 4.3 scatter_custom_fusion
  254.0 0.1 reshape.85
  254.1 20.9 %all_to_all.26 = s32[64,2,16]{2,1,0:T(2,128)S(1)} all-to-all(s32[64,2,16]{2,1,0:T(2,128)S(1)} %reshape.85), channel_id=1, replica_groups=mesh['segment'=8,'vocab'=64] {'vocab'}, dimensions={0} | all-to-all | bytes 16384 | tf_op jit(solution)/shard_map/all_to_all | solution.py:56
  275.0 130.8 %all-gather.3.cloned.1.call-done = f32[512,2,16,512]{3,2,0,1:T(8,128)} async-done(((f32[64,2,16,512]{3,2,0,1:T(8,128)}), f32[512,2,16,512]{3,2,0,1:T(8,128)}) %all-gather.3.cloned.1.call-update) | async-done | bytes 33554448 | tf_op jit(solution)/shard_map/all_gather | solution.py:12
  405.8 15.1 %reduce_sum.68 = f32[64,2,16,512]{3,2,0,1:T(8,128)} reduce(f32[8,64,2,16,512]{4,3,1,0,2:T(8,128)} %bitcast.36, f32[]{:T(128)} %constant.15.clone.1), dimensions={0}, to_apply=%region_7.8 | reduce | flops 7340032 | bytes 37748740 | tf_op jit(solution)/shard_map/reduce_sum | solution.py:13
  421.0 2.5 reduce_max.18
  423.5 3.2 exponential_reduce_fusion
  426.7 0.7 copy.36
  427.4 15.6 %all-to-all-start.4 = ((f32[64,2,16]{2,1,0:T(2,128)}), f32[64,2,16]{2,1,0:T(2,128)S(1)}, u32[]{:S(2)}, u32[]{:S(2)}) async-start(f32[64,2,16]{2,1,0:T(2,128)} %copy.36), calls=%async_computation.4 | async-start | bytes 131072 | tf_op jit(solution)/shard_map/all_to_all | solution.py:72
  443.0 0.7 copy.35
  443.6 14.8 %all-to-all-done.4 = f32[64,2,16]{2,1,0:T(2,128)S(1)} async-done(((f32[64,2,16]{2,1,0:T(2,128)}), f32[64,2,16]{2,1,0:T(2,128)S(1)}, u32[]{:S(2)}, u32[]{:S(2)}) %all-to-all-start.4) | async-done | bytes 8224 | tf_op jit(solution)/shard_map/all_to_all | solution.py:72
  458.4 4.8 all-to-all-start.3
  463.2 0.7 copy.34
  463.9 14.6 %all-to-all-done.3 = f32[64,2,16]{2,1,0:T(2,128)S(1)} async-done(((f32[64,2,16]{2,1,0:T(2,128)}), f32[64,2,16]{2,1,0:T(2,128)S(1)}, u32[]{:S(2)}, u32[]{:S(2)}) %all-to-all-start.3) | async-done | bytes 8224 | tf_op jit(solution)/shard_map/all_to_all | solution.py:71
  478.5 4.6 all-to-all-start.2
  483.1 0.1 reshape.92
  483.2 6.2 %gather_fusion.3 = f32[1024]{0:T(1024)S(1)} fusion(f32[2048]{0:T(1024)S(1)} %reshape.92, s32[1024]{0:T(1024)S(1)} %broadcast_clamp_fusion), kind=kCustom, calls=%fused_computation.3 | custom fusion | bytes 12288 | tf_op jit(solution)/shard_map/gather | solution.py:76
  489.4 0.1 reshape.90
  489.5 6.2 %gather_fusion.2 = f32[1024]{0:T(1024)S(1)} fusion(f32[2048]{0:T(1024)S(1)} %reshape.90, s32[1024]{0:T(1024)S(1)} %broadcast_clamp_fusion), kind=kCustom, calls=%fused_computation.2 | custom fusion | bytes 12288 | tf_op jit(solution)/shard_map/gather | solution.py:75
  495.7 2.6 all-to-all-done.2
  498.3 0.1 reshape.88
  498.4 6.2 %gather_fusion.1 = f32[1024]{0:T(1024)S(1)} fusion(f32[2048]{0:T(1024)S(1)} %reshape.88, s32[1024]{0:T(1024)S(1)} %broadcast_clamp_fusion), kind=kCustom, calls=%fused_computation.1 | custom fusion | bytes 12288 | tf_op jit(solution)/shard_map/gather | solution.py:77
  504.6 0.6 add_subtract_fusion
  (21 shorter events, 0.3 us)
Async XLA Ops:
  6.5 238.0 %copy-start = (bf16[1024,1024]{1,0:T(8,128)(2,1)S(1)}, bf16[1024,1024]{1,0:T(8,128)(2,1)}, u32[]{:S(2)}) copy-start(bf16[1024,1024]{1,0:T(8,128)(2,1)} %param.8) | copy-start | bytes 6291460
  6.5 23.5 %copy-start.1 = (bf16[256,1024]{1,0:T(8,128)(2,1)S(1)}, bf16[256,1024]{1,0:T(8,128)(2,1)}, u32[]{:S(2)}) copy-start(bf16[256,1024]{1,0:T(8,128)(2,1)} %param.6) | copy-start | bytes 1572868
  6.5 399.3 %all-gather.3.cloned.1.call-start = ((), (), s32[]{:S(2)}) async-start(), calls=%async_computation.5 | async-start | bytes 37748736 | tf_op jit(solution)/shard_map/all_gather | solution.py:12
  249.0 0.7 copy-start.2
  249.0 0.7 copy-start.3
  427.4 31.1 %all-to-all-start.4 = ((f32[64,2,16]{2,1,0:T(2,128)}), f32[64,2,16]{2,1,0:T(2,128)S(1)}, u32[]{:S(2)}, u32[]{:S(2)}) async-start(f32[64,2,16]{2,1,0:T(2,128)} %copy.36), calls=%async_computation.4 | async-start | bytes 131072 | tf_op jit(solution)/shard_map/all_to_all | solution.py:72
  458.4 20.1 %all-to-all-start.3 = ((f32[64,2,16]{2,1,0:T(2,128)}), f32[64,2,16]{2,1,0:T(2,128)S(1)}, u32[]{:S(2)}, u32[]{:S(2)}) async-start(f32[64,2,16]{2,1,0:T(2,128)} %copy.35), calls=%async_computation.3 | async-start | bytes 131072 | tf_op jit(solution)/shard_map/all_to_all | solution.py:71
  478.5 19.8 %all-to-all-start.2 = ((f32[64,2,16]{2,1,0:T(2,128)}), f32[64,2,16]{2,1,0:T(2,128)S(1)}, u32[]{:S(2)}, u32[]{:S(2)}) async-start(f32[64,2,16]{2,1,0:T(2,128)} %copy.34), calls=%async_computation.2 | async-start | bytes 131072 | tf_op jit(solution)/shard_map/all_to_all | solution.py:73
Sparse Core Ops, SparseCore 0:
  249.1 156.6 all-gather.2
